TPU v7x, 32 devices: a whole 2x2x4 slice. The times are simulated.
32 devices in a mesh: group: 2 (over y), role: 2 (over core), dev: 8 (over z, x).
Axes of the slice: x: 2, y: 2, z: 4, core: 2. Of those that a mesh axis runs over, the one named last changes fastest.
Arguments:
- hidden: bfloat16 [64, 7168], P(('group', 'role', 'dev')), parts along dimension 0, may hold values from -6 to 6
- norm_gain: bfloat16 [7168], replicated, may hold values from 0.099609375 to 1.8984375
- routes: int32 [64, 8], P(('group', 'role', 'dev')), parts along dimension 0, may hold values from 0 to 15, all different within a row; in each aligned block of 2 rows (0 to 1, 2 to 3, ...) at most 2 rows name the same one
- gate_weights: float32 [64, 8], P(('group', 'role', 'dev')), parts along dimension 0, may hold values from 0.1 to 0.5
- w_gate: bfloat16 [7168, 32768], P(None, ('role', 'dev')), may hold values from -0.0625 to 0.0625
- w_up: bfloat16 [7168, 32768], P(None, ('role', 'dev')), may hold values from -0.0625 to 0.0625
- w_down: bfloat16 [32768, 7168], P(('role', 'dev')), may hold values from -0.125 to 0.125
- queries: bfloat16 [64, 64, 576], P(('group', 'role', 'dev')), parts along dimension 0, may hold values from -48 to 48
- local_cache: bfloat16 [64, 64, 576], P(('group', 'role', 'dev')), parts along dimension 0, may hold values from -6 to 6
- cache_lengths: int32 [64], P(('group', 'role', 'dev')), parts along dimension 0, may hold values from 2 to 64
- swap_pool: bfloat16 [512, 16, 576], P(('group', 'role', 'dev')), parts along dimension 0, may hold values from -6 to 6
- page_ids: int32 [32, 16], P(('group', 'role', 'dev')), parts along dimension 0, may hold values from 0 to 15
- page_owner: int32 [32, 16], P(('group', 'role', 'dev')), parts along dimension 0, may hold values from 0 to 1
Outputs:
- attn_out: bfloat16 [64, 64, 512], P(('group', 'role', 'dev')), parts along dimension 0
- moe_out: bfloat16 [64, 7168], P(('group', 'role', 'dev')), parts along dimension 0
There are 2 independent parts, one for each index of `group`. A program takes and returns all parts, laid end to end along the dimension named above; an argument that names none is the same for every part. Nothing has to cross between parts.
Inputs may be any that keep to these rules, and one draw needn't show every extreme that they name: `routes`: each row names 8 different experts; in the rows of one device no expert is named more than 2 times. `page_ids`: every device receives exactly one page from every holder.
All inputs are finite; a program needn't handle non-finite values.
Results may differ from a plain program's by a relative error of at most 0.0046.
Values may be sent and summed in bfloat16 or wider, within the bound.
A program may use at most 128 MiB of HBM per device.

v0:
```python
import jax
import jax.numpy as jnp
from jax import lax
from jax.sharding import PartitionSpec as P

ROPE = 64
EXPERTS = 16


score_scale = 192.0 ** (-0.5)
norm_eps = 1e-06


def device_attention(queries, local_cache, cache_lengths, fetched, owners):
    local_scores = (
        jnp.einsum("rhc,rtc->rht", queries, local_cache, preferred_element_type=jnp.float32)
        * score_scale
    )
    positions = jnp.arange(local_cache.shape[1], dtype=jnp.int32)
    local_valid = positions[None, None, :] < cache_lengths[:, None, None]
    local_scores = jnp.where(local_valid, local_scores, -jnp.inf)
    page_query = queries[owners]
    page_scores = (
        jnp.einsum("phc,ptc->pht", page_query, fetched, preferred_element_type=jnp.float32)
        * score_scale
    )
    request_ids = jnp.arange(queries.shape[0], dtype=jnp.int32)
    belongs = owners[None, :] == request_ids[:, None]
    page_peak = jnp.max(page_scores, axis=2)
    owned_peak = jnp.max(jnp.where(belongs[:, :, None], page_peak[None], -jnp.inf), axis=1)
    row_peak = jnp.maximum(jnp.max(local_scores, axis=2), owned_peak)
    local_exp = jnp.exp(local_scores - row_peak[:, :, None])
    page_exp = jnp.exp(page_scores - row_peak[owners][:, :, None])
    page_total = jnp.sum(page_exp, axis=2)
    owned_total = jnp.sum(jnp.where(belongs[:, :, None], page_total[None], 0.0), axis=1)
    normalizer = jnp.sum(local_exp, axis=2) + owned_total
    local_probs = (local_exp / normalizer[:, :, None]).astype(jnp.bfloat16)
    page_probs = (page_exp / normalizer[owners][:, :, None]).astype(jnp.bfloat16)
    value_width = queries.shape[2] - ROPE
    local_part = jnp.einsum(
        "rht,rtc->rhc",
        local_probs,
        local_cache[:, :, :value_width],
        preferred_element_type=jnp.float32,
    )
    page_part = jnp.einsum(
        "pht,ptc->phc", page_probs, fetched[:, :, :value_width], preferred_element_type=jnp.float32
    )
    owned_part = jnp.einsum(
        "rp,phc->rhc", belongs.astype(jnp.float32), page_part, precision=lax.Precision.HIGHEST
    )
    return (local_part + owned_part).astype(jnp.bfloat16)


def expert_block(slot_rows, w_gate, w_up, w_down):
    flat_rows = slot_rows.reshape(-1, slot_rows.shape[-1])
    gate_proj = jnp.dot(flat_rows, w_gate, preferred_element_type=jnp.float32)
    up_proj = jnp.dot(flat_rows, w_up, preferred_element_type=jnp.float32)
    act_units = (jax.nn.silu(gate_proj) * up_proj).astype(jnp.bfloat16)
    output = jnp.dot(act_units, w_down, preferred_element_type=jnp.float32)
    return output.reshape(slot_rows.shape[:-1] + (w_down.shape[1],))


def slot_table(route_codes, expert_ids, capacity):
    is_routed = jnp.any(route_codes[:, :, None, :] == expert_ids[None, None, :, None], axis=3)
    routed_int = is_routed.astype(jnp.int32)
    before = jnp.cumsum(routed_int, axis=1) - routed_int
    slot_ids = jnp.arange(capacity, dtype=jnp.int32)
    chosen = is_routed[:, :, :, None] & (before[:, :, :, None] == slot_ids[None, None, None, :])
    return jnp.transpose(chosen, (0, 2, 3, 1)).astype(jnp.bfloat16)


def per_device(
    hidden,
    norm_gain,
    routes,
    gate_weights,
    w_gate,
    w_up,
    w_down,
    queries,
    local_cache,
    cache_lengths,
    swap_pool,
    page_ids,
    page_owner,
):
    devices = lax.axis_size(("role", "dev"))
    slices = devices // EXPERTS
    row_count = hidden.shape[0]
    width = hidden.shape[1]
    capacity = row_count // 2 + 1
    wanted = lax.all_to_all(
        page_ids.reshape(-1), ("role", "dev"), split_axis=0, concat_axis=0, tiled=True
    )
    outgoing = swap_pool[wanted]
    arrived = lax.all_to_all(outgoing, ("role", "dev"), split_axis=0, concat_axis=0, tiled=True)
    attn_out = device_attention(
        queries, local_cache, cache_lengths, arrived, page_owner.reshape(-1)
    )
    hidden_wide = hidden.astype(jnp.float32)
    inv_rms = lax.rsqrt(jnp.mean(hidden_wide * hidden_wide, axis=1, keepdims=True) + norm_eps)
    normed = (hidden_wide * inv_rms * norm_gain.astype(jnp.float32)[None, :]).astype(jnp.bfloat16)
    expert_ids = jnp.arange(EXPERTS, dtype=jnp.int32)
    own_table = slot_table(routes[None], expert_ids, capacity)[0]
    per_expert = jnp.einsum(
        "ecr,rd->ecd", own_table, normed, preferred_element_type=jnp.float32
    ).astype(jnp.bfloat16)
    spread = jnp.broadcast_to(per_expert[:, None], (EXPERTS, slices, capacity, width)).reshape(
        devices, capacity, width
    )
    partial_out = expert_block(
        lax.all_to_all(spread, ("role", "dev"), split_axis=0, concat_axis=0, tiled=True),
        w_gate,
        w_up,
        w_down,
    )
    returned = lax.all_to_all(partial_out, ("role", "dev"), split_axis=0, concat_axis=0, tiled=True)
    summed = jnp.sum(returned.reshape(EXPERTS, slices, capacity, width), axis=1)
    route_weight = jnp.sum(
        jnp.where(routes[:, :, None] == expert_ids[None, None, :], gate_weights[:, :, None], 0.0),
        axis=1,
    )
    mixing = own_table.astype(jnp.float32) * jnp.transpose(route_weight)[:, None, :]
    combined = jnp.einsum("ecr,ecd->rd", mixing, summed, precision=lax.Precision.HIGHEST)
    moe_out = (hidden_wide + combined).astype(jnp.bfloat16)
    return (attn_out, moe_out)


def solution(mesh):
    in_specs = (
        P(("group", "role", "dev"), None),
        P(),
        P(("group", "role", "dev"), None),
        P(("group", "role", "dev"), None),
        P(None, ("role", "dev")),
        P(None, ("role", "dev")),
        P(("role", "dev"), None),
        P(("group", "role", "dev"), None, None),
        P(("group", "role", "dev"), None, None),
        P(("group", "role", "dev")),
        P(("group", "role", "dev"), None, None),
        P(("group", "role", "dev"), None),
        P(("group", "role", "dev"), None),
    )
    out_specs = (P(("group", "role", "dev"), None, None), P(("group", "role", "dev"), None))
    return jax.shard_map(
        per_device, mesh=mesh, in_specs=in_specs, out_specs=out_specs, check_vma=False
    )
```

profile of v0, /device:TPU:0, one launch (start us, length us, event | category | flops | bytes accessed | tf_op | source)
XLA Modules:
  0.0 107.0 jit_solution(9635600186236785544)
XLA Ops:
  0.6 1.4 %copy.34 = s32[16,1,1]{2,1,0:T(1,128)} copy(s32[16,1,1]{0,2,1:T(1,128)} %bitcast.44) | data formatting | bytes 128 | tf_op jit(solution)/shard_map/all_to_all | solution.py:93
  2.0 7.4 %all-to-all-start = ((s32[16,1,1]{2,1,0:T(1,128)}), s32[16,1,1]{2,1,0:T(1,128)S(1)}, u32[]{:S(2)}, u32[]{:S(2)}) async-start(s32[16,1,1]{2,1,0:T(1,128)} %copy.34), calls=%async_computation | async-start | bytes 16384 | tf_op jit(solution)/shard_map/all_to_all | solution.py:93
  9.4 0.7 fusion.38
  10.1 0.8 fusion.29
  10.9 0.7 convert_element_type.61
  11.6 0.9 fusion.22
  12.5 1.1 %convolution_convert_fusion = bf16[16,2,7168]{2,0,1:T(8,128)(2,1)S(1)} fusion(bf16[2,7168]{1,0:T(2,128)(2,1)} %param.13, f32[2]{0:T(128)S(1)} %add_rsqrt_fusion, f32[7168]{0:T(1024)S(1)} %convert_element_type.61, pred[2,16]{1,0:T(4,128)(4,1)S(1)} %fusion.29, s32[2,16]{1,0:T(2,128)S(1)} %convert_subtract_fusion), kind=kOutput, calls=%fused_computation.4 | convolution fusion | flops 1204352 | bytes 516264 | tf_op jit(solution)/shard_map/ecr,rd->ecd/dot_general | solution.py:106
  13.6 1.2 %copy.38 = bf16[16,2,7168]{2,1,0:T(2,128)(2,1)} copy(bf16[16,2,7168]{2,0,1:T(8,128)(2,1)S(1)} %convolution_convert_fusion) | data formatting | bytes 917504 | tf_op jit(solution)/shard_map/convert_element_type | solution.py:108
  14.9 1.7 %gather_fusion = bf16[16,64,576]{2,1,0:T(8,128)(2,1)S(1)} fusion(bf16[2,64,576]{2,1,0:T(8,128)(2,1)} %param.20, s32[1024]{0:T(1024)S(1)} %pad_clamp_fusion.1), kind=kCustom, calls=%fused_computation | custom fusion | bytes 2359360 | tf_op jit(solution)/shard_map/gather | solution.py:22
  16.6 6.0 %all-to-all-start.2 = ((bf16[16,2,7168]{2,1,0:T(2,128)(2,1)}), bf16[16,2,7168]{2,1,0:T(2,128)(2,1)S(1)}, u32[]{:S(2)}, u32[]{:S(2)}) async-start(bf16[16,2,7168]{2,1,0:T(2,128)(2,1)} %copy.38), calls=%async_computation.2 | async-start | bytes 917504 | tf_op jit(solution)/shard_map/all_to_all | solution.py:113
  22.6 0.8 select_reduce_fusion.2
  23.4 0.7 iota_compare_fusion.3
  24.1 1.2 %fusion.41 = (f32[2,64]{1,0:T(2,128)S(1)}, f32[2,64,64]{1,2,0:T(8,128)S(1)}) fusion(bf16[2,64,576]{2,1,0:T(8,128)(2,1)} %param.20, bf16[2,64,576]{2,1,0:T(8,128)(2,1)} %param.21, pred[2,64]{1,0:T(4,128)(4,1)S(1)} %iota_compare_fusion.3), kind=kOutput, calls=%fused_computation.71 | convolution fusion | flops 9461632 | bytes 328320 | tf_op jit(solution)/shard_map/rhc,rtc->rht/dot_general | solution.py:16
  25.8 1.3 %gather_fusion.1 = bf16[16,16,576]{2,1,0:T(8,128)(2,1)} fusion(bf16[16,16,576]{2,1,0:T(8,128)(2,1)S(1)} %copy-done, s32[1024]{0:T(1024)S(1)} %pad_clamp_fusion), kind=kCustom, calls=%fused_computation.1 | custom fusion | bytes 589888 | tf_op jit(solution)/shard_map/gather | solution.py:96
  27.1 10.0 %all-to-all-done.2 = bf16[16,2,7168]{2,1,0:T(2,128)(2,1)S(1)} async-done(((bf16[16,2,7168]{2,1,0:T(2,128)(2,1)}), bf16[16,2,7168]{2,1,0:T(2,128)(2,1)S(1)}, u32[]{:S(2)}, u32[]{:S(2)}) %all-to-all-start.2) | async-done | bytes 458784 | tf_op jit(solution)/shard_map/all_to_all | solution.py:113
  37.1 3.5 %all-to-all-start.1 = ((bf16[16,16,576]{2,1,0:T(8,128)(2,1)}), bf16[16,16,576]{2,1,0:T(8,128)(2,1)S(1)}, u32[]{:S(2)}, u32[]{:S(2)}) async-start(bf16[16,16,576]{2,1,0:T(8,128)(2,1)} %gather_fusion.1), calls=%async_computation.1 | async-start | bytes 655360 | tf_op jit(solution)/shard_map/all_to_all | solution.py:97
  40.8 12.7 %fusion.43 = f32[32,2048]{1,0:T(8,128)} fusion(bf16[32,7168]{1,0:T(8,128)(2,1)S(1)} %reshape.196, bf16[7168,2048]{1,0:T(8,128)(2,1)} %param.17), kind=kOutput, calls=%fused_computation.73 | convolution fusion | flops 939524096 | bytes 30081024 | tf_op jit(solution)/shard_map/dot_general | solution.py:57
  53.5 20.8 %fusion.3 = f32[32,7168]{1,0:T(8,128)S(1)} fusion(bf16[2048,7168]{1,0:T(8,128)(2,1)} %param.19, bf16[32,7168]{1,0:T(8,128)(2,1)S(1)} %reshape.196, bf16[7168,2048]{1,0:T(8,128)(2,1)} %param.18, f32[32,2048]{1,0:T(8,128)} %fusion.43), kind=kOutput, calls=%fused_computation.10 | convolution fusion | flops 1879441408 | bytes 60358656 | tf_op jit(solution)/shard_map/dot_general | solution.py:60
  74.3 1.5 %reshape.197 = f32[16,2,7168]{2,1,0:T(2,128)} reshape(f32[32,7168]{1,0:T(8,128)S(1)} %fusion.3) | data formatting | bytes 1835008 | tf_op jit(solution)/shard_map/reshape | solution.py:61
  75.8 5.9 %all-to-all-start.3 = ((f32[16,2,7168]{2,1,0:T(2,128)}), f32[16,2,7168]{2,1,0:T(2,128)S(1)}, u32[]{:S(2)}, u32[]{:S(2)}) async-start(f32[16,2,7168]{2,1,0:T(2,128)} %reshape.197), calls=%async_computation.3 | async-start | bytes 1835008 | tf_op jit(solution)/shard_map/all_to_all | solution.py:118
  84.2 2.0 %fusion.4 = f32[2,64,512]{2,0,1:T(2,128)S(1)} fusion(f32[16,64,512]{2,1,0:T(8,128)S(1)} %fusion.9, s32[16]{0:T(128)S(1)} %bitcast.43), kind=kOutput, calls=%fused_computation.11 | convolution fusion | flops 12582944 | bytes 2359360 | tf_op jit(solution)/shard_map/rp,phc->rhc/dot_general | solution.py:49
  86.2 1.8 %fusion.6 = bf16[2,64,512]{2,1,0:T(8,128)(2,1)} fusion(f32[2,64,512]{2,0,1:T(2,128)S(1)} %fusion.4, bf16[2,64,576]{2,1,0:T(8,128)(2,1)} %param.21, f32[2,64,64]{1,2,0:T(8,128)S(1)} %get-tuple-element.3, f32[2,64]{1,0:T(2,128)S(1)} %add.49, f32[2,64]{1,0:T(2,128)S(1)} %max.7), kind=kOutput, calls=%fused_computation.14 | convolution fusion | flops 8544256 | bytes 558080 | tf_op jit(solution)/shard_map/rht,rtc->rhc/dot_general | solution.py:40
  88.0 17.6 %all-to-all-done.3 = f32[16,2,7168]{2,1,0:T(2,128)S(1)} async-done(((f32[16,2,7168]{2,1,0:T(2,128)}), f32[16,2,7168]{2,1,0:T(2,128)S(1)}, u32[]{:S(2)}, u32[]{:S(2)}) %all-to-all-start.3) | async-done | bytes 917536 | tf_op jit(solution)/shard_map/all_to_all | solution.py:118
  105.6 1.4 %fusion.1 = bf16[2,7168]{1,0:T(2,128)(2,1)} fusion(f32[16,2,7168]{2,1,0:T(2,128)S(1)} %all-to-all-done.3, bf16[2,7168]{1,0:T(2,128)(2,1)S(1)} %copy-done.1, pred[2,16]{1,0:T(4,128)(4,1)S(1)} %fusion.29, f32[16,2]{0,1:T(2,128)S(1)} %bitcast.41, s32[2,16]{1,0:T(2,128)S(1)} %convert_subtract_fusion), kind=kOutput, calls=%fused_computation.7 | convolution fusion | flops 5548352 | bytes 975136 | tf_op jit(solution)/shard_map/ecr,ecd->rd/dot_general | solution.py:125
  (28 shorter events, 3.1 us)
Async XLA Ops:
  0.6 25.1 %copy-start = (bf16[16,16,576]{2,1,0:T(8,128)(2,1)S(1)}, bf16[16,16,576]{2,1,0:T(8,128)(2,1)}, u32[]{:S(2)}) copy-start(bf16[16,16,576]{2,1,0:T(8,128)(2,1)} %param.23) | copy-start | bytes 884740
  2.0 14.6 %all-to-all-start = ((s32[16,1,1]{2,1,0:T(1,128)}), s32[16,1,1]{2,1,0:T(1,128)S(1)}, u32[]{:S(2)}, u32[]{:S(2)}) async-start(s32[16,1,1]{2,1,0:T(1,128)} %copy.34), calls=%async_computation | async-start | bytes 16384 | tf_op jit(solution)/shard_map/all_to_all | solution.py:93
  16.6 20.5 %all-to-all-start.2 = ((bf16[16,2,7168]{2,1,0:T(2,128)(2,1)}), bf16[16,2,7168]{2,1,0:T(2,128)(2,1)S(1)}, u32[]{:S(2)}, u32[]{:S(2)}) async-start(bf16[16,2,7168]{2,1,0:T(2,128)(2,1)} %copy.38), calls=%async_computation.2 | async-start | bytes 917504 | tf_op jit(solution)/shard_map/all_to_all | solution.py:113
  37.1 38.7 %all-to-all-start.1 = ((bf16[16,16,576]{2,1,0:T(8,128)(2,1)}), bf16[16,16,576]{2,1,0:T(8,128)(2,1)S(1)}, u32[]{:S(2)}, u32[]{:S(2)}) async-start(bf16[16,16,576]{2,1,0:T(8,128)(2,1)} %gather_fusion.1), calls=%async_computation.1 | async-start | bytes 655360 | tf_op jit(solution)/shard_map/all_to_all | solution.py:97
  53.5 28.2 %copy-start.2 = (s32[1,16]{1,0:T(1,128)S(1)}, s32[1,16]{1,0:T(1,128)}, u32[]{:S(2)}) copy-start(s32[1,16]{1,0:T(1,128)} %param.25) | copy-start | bytes 196
  53.5 52.1 %copy-start.1 = (bf16[2,7168]{1,0:T(2,128)(2,1)S(1)}, bf16[2,7168]{1,0:T(2,128)(2,1)}, u32[]{:S(2)}) copy-start(bf16[2,7168]{1,0:T(2,128)(2,1)} %param.13) | copy-start | bytes 86020
  75.8 29.8 %all-to-all-start.3 = ((f32[16,2,7168]{2,1,0:T(2,128)}), f32[16,2,7168]{2,1,0:T(2,128)S(1)}, u32[]{:S(2)}, u32[]{:S(2)}) async-start(f32[16,2,7168]{2,1,0:T(2,128)} %reshape.197), calls=%async_computation.3 | async-start | bytes 1835008 | tf_op jit(solution)/shard_map/all_to_all | solution.py:118
where the time goes:
time: 108 us; the launch traced here: 107 us
  matrix products  42.1 us (39%)
  waiting for transfers between devices  27.6 us (26%)
  starting transfers between devices  22.8 us (21%)
  local copies, waits for them, and re-layouts  8.41 us (8%)
  other arithmetic  5.31 us (5%)
    dot_general x1, matrix products, expert_block(): output = jnp.dot(act_units, w_down, preferred_element_type=jnp.float32)  20.8 us
    all_to_all x1, waiting for transfers between devices, per_device(): lax.all_to_all(partial_out, ('role', 'dev'), split_axis=0, concat_axis=0,...  17.6 us
    dot_general x1, matrix products, expert_block(): gate_proj = jnp.dot(flat_rows, w_gate, preferred_element_type=jnp.float32)  12.7 us
    all_to_all x1, waiting for transfers between devices, per_device(): lax.all_to_all(spread, ('role', 'dev'), split_axis=0, concat_axis=0, tile...  10 us
    all_to_all x1, starting transfers between devices, per_device(): lax.all_to_all(page_ids.reshape(-1), ('role', 'dev'), split_axis=0, conca...  7.36 us
    all_to_all x1, starting transfers between devices, per_device(): lax.all_to_all(spread, ('role', 'dev'), split_axis=0, concat_axis=0, tile...  6.02 us
    all_to_all x1, starting transfers between devices, per_device(): lax.all_to_all(partial_out, ('role', 'dev'), split_axis=0, concat_axis=0,...  5.92 us
    all_to_all x1, starting transfers between devices, per_device(): lax.all_to_all(outgoing, ('role', 'dev'), split_axis=0, concat_axis=0, ti...  3.54 us
  transfers between devices with their start and end apart: 4, of which 2 were waited for; matrix products, arithmetic and copies ran while one was open for 49% of the time, Pallas kernels for 0%

commit v1 on v0

v1 whole, which is shorter than its diff:
```python
import functools

import jax
import jax.numpy as jnp
from jax import lax
from jax.experimental import pallas as pl
from jax.experimental.pallas import tpu as pltpu
from jax.sharding import PartitionSpec as P

ROPE = 64
EXPERTS = 16
TILE = 16
LANES = 128
AHEAD = 4


score_scale = 192.0 ** (-0.5)
norm_eps = 1e-06


def iota(shape, axis):
    return lax.broadcasted_iota(jnp.int32, shape, axis)


def div(value, power):
    return value >> (power.bit_length() - 1)


def mod(value, power):
    return value & (power - 1)


def layer_kernel(
    sizes,
    hidden_ref,
    gain_ref,
    ids_ref,
    routes_ref,
    mix_ref,
    lengths_ref,
    owner_ref,
    queries_hbm,
    cache_hbm,
    pool_hbm,
    gate_hbm,
    up_hbm,
    down_hbm,
    attn_ref,
    moe_ref,
    gate_buf,
    up_buf,
    down_buf,
    queries_buf,
    cache_buf,
    pool_buf,
    packed,
    row_send,
    row_recv,
    row_parts,
    gate_acc,
    up_acc,
    units,
    ids_send,
    ids_recv,
    page_send,
    page_recv,
    out_send,
    out_recv,
    out_wide,
    gate_sem,
    up_sem,
    down_sem,
    small_sem,
    ids_sems,
    row_sems,
    page_sems,
    out_send_sem,
    out_recv_sem,
):
    roles, devs = sizes
    n = roles * devs
    rows, width = hidden_ref.shape
    subs = TILE // rows
    part = width // subs
    chunk = subs * LANES
    chunks = width // chunk
    block = min(n, 16)
    block_rows = block * rows
    me = lax.axis_index("role") * devs + lax.axis_index("dev")

    def target(step):
        peer = lax.rem(me + step, n)
        return peer, {"role": peer // devs, "dev": lax.rem(peer, devs)}

    def gate_copy(s):
        return pltpu.make_async_copy(
            gate_hbm.at[pl.ds(s * part, part), :],
            gate_buf.at[lax.rem(s, AHEAD)],
            gate_sem.at[lax.rem(s, AHEAD)],
        )

    def up_copy(s):
        return pltpu.make_async_copy(
            up_hbm.at[pl.ds(s * part, part), :],
            up_buf.at[lax.rem(s, AHEAD)],
            up_sem.at[lax.rem(s, AHEAD)],
        )

    def down_copy(c):
        return pltpu.make_async_copy(
            down_hbm.at[:, pl.ds(pl.multiple_of(c * chunk, chunk), chunk)],
            down_buf.at[c],
            down_sem.at[c],
        )

    small = [
        pltpu.make_async_copy(source, dest, small_sem.at[i])
        for i, (source, dest) in enumerate(
            ((pool_hbm, pool_buf), (queries_hbm, queries_buf), (cache_hbm, cache_buf))
        )
    ]
    barrier = pltpu.get_barrier_semaphore()

    def greet(step, carry):
        _, device = target(step)
        pl.semaphore_signal(barrier, inc=1, device_id=device, device_id_type=pl.DeviceIdType.MESH)
        return carry

    lax.fori_loop(1, n, greet, 0)
    for copy in small:
        copy.start()

    def first_weights(s, carry):
        gate_copy(s).start()
        up_copy(s).start()
        return carry

    lax.fori_loop(0, AHEAD, first_weights, 0)
    early = min(2, chunks)
    for c in range(early):
        down_copy(c).start()

    ids_send[...] = jnp.zeros_like(ids_send)
    ids_send[:, 0:n] = jnp.broadcast_to(ids_ref[...], (8, n))
    hidden_wide = hidden_ref[...].astype(jnp.float32)
    inv_rms = lax.rsqrt(jnp.mean(hidden_wide * hidden_wide, axis=1, keepdims=True) + norm_eps)
    normed = hidden_wide * inv_rms * gain_ref[...].astype(jnp.float32)
    for r in range(rows):
        for s in range(subs):
            packed[r * subs + s : r * subs + s + 1, :] = normed[r : r + 1, s * part : (s + 1) * part]
    row_send[...] = packed[...].astype(jnp.bfloat16)
    own = pl.ds(pl.multiple_of(me * TILE, TILE), TILE)
    row_recv[own, :] = row_send[...]
    ids_recv[me] = ids_send[...]
    pl.semaphore_wait(barrier, n - 1)

    def send_all(source_of, dest, send_sem, recv_sem):
        def send(step, carry):
            peer, device = target(step)
            pltpu.make_async_remote_copy(
                src_ref=source_of(peer),
                dst_ref=dest,
                send_sem=send_sem,
                recv_sem=recv_sem,
                device_id=device,
                device_id_type=pl.DeviceIdType.MESH,
            ).start()
            return carry

        lax.fori_loop(1, n, send, 0)

    def wait_all(ref, sem):
        pltpu.make_async_copy(ref, ref, sem).wait()

    others = pl.ds(0, (n - 1) * TILE)
    send_all(lambda peer: ids_send, ids_recv.at[me], ids_sems.at[0], ids_sems.at[1])
    send_all(lambda peer: row_send, row_recv.at[own, :], row_sems.at[0], row_sems.at[1])

    def peer_rows(peer):
        return pl.ds(pl.multiple_of(peer * TILE, TILE), TILE)

    small[0].wait()
    wait_all(ids_recv.at[pl.ds(0, n - 1)], ids_sems.at[1])
    ids_all = ids_recv[...]
    wanted = jnp.sum(jnp.where(iota(ids_all.shape, 2) == me, ids_all, 0), axis=2, keepdims=True)
    wanted = jnp.concatenate([wanted, wanted], axis=1).reshape(n * TILE, 1)
    pool_rows = pool_buf[...].reshape(-1, pool_buf.shape[2])
    pick = (n * TILE, pool_rows.shape[0])
    chosen = (wanted == div(iota(pick, 1), TILE)) & (
        mod(iota(pick, 0), TILE) == mod(iota(pick, 1), TILE)
    )
    page_send[...] = jnp.dot(
        jnp.where(chosen, 1.0, 0.0).astype(jnp.bfloat16),
        pool_rows,
        preferred_element_type=jnp.float32,
    ).astype(jnp.bfloat16)
    send_all(
        lambda peer: page_send.at[peer_rows(peer), :],
        page_recv.at[own, :],
        page_sems.at[0],
        page_sems.at[1],
    )
    page_recv[own, :] = page_send[own, :]

    square = (block * TILE, block * TILE)

    def place(index):
        return mod(index, block_rows) * subs + div(index, block_rows)

    to_parts = jnp.where(place(iota(square, 0)) == iota(square, 1), 1.0, 0.0).astype(jnp.bfloat16)
    to_packed = jnp.where(iota(square, 0) == place(iota(square, 1)), 1.0, 0.0).astype(jnp.bfloat16)

    wait_all(row_recv.at[others, :], row_sems.at[1])
    for b in range(n // block):
        moved = jnp.dot(
            to_parts,
            row_recv[b * block * TILE : (b + 1) * block * TILE, :],
            preferred_element_type=jnp.float32,
        ).astype(jnp.bfloat16)
        for s in range(subs):
            row_parts[s, b * block_rows : (b + 1) * block_rows, :] = moved[
                s * block_rows : (s + 1) * block_rows, :
            ]

    gate_acc[...] = jnp.zeros_like(gate_acc)
    up_acc[...] = jnp.zeros_like(up_acc)

    def project(s, carry):
        slot = lax.rem(s, AHEAD)
        x = row_parts[s]
        gate_copy(s).wait()
        gate_acc[...] += jnp.dot(x, gate_buf[slot], preferred_element_type=jnp.float32)
        up_copy(s).wait()
        up_acc[...] += jnp.dot(x, up_buf[slot], preferred_element_type=jnp.float32)

        @pl.when(s + AHEAD < subs)
        def _():
            gate_copy(s + AHEAD).start()
            up_copy(s + AHEAD).start()

        @pl.when(s == max(subs - AHEAD - 1, 0))
        def _():
            for c in range(early, chunks):
                down_copy(c).start()

        return carry

    lax.fori_loop(0, subs, project, 0)
    gate = gate_acc[...]
    units[...] = (gate / (1.0 + jnp.exp(-gate)) * up_acc[...]).astype(jnp.bfloat16)

    def expand(c, carry):
        down_copy(c).wait()
        partial = jnp.dot(units[...], down_buf[c], preferred_element_type=jnp.float32).astype(
            jnp.bfloat16
        )
        for b in range(n // block):
            stacked = jnp.concatenate(
                [
                    partial[b * block_rows : (b + 1) * block_rows, q * LANES : (q + 1) * LANES]
                    for q in range(subs)
                ],
                axis=0,
            )
            out_send[c, b * block * TILE : (b + 1) * block * TILE, :] = jnp.dot(
                to_packed, stacked, preferred_element_type=jnp.float32
            ).astype(jnp.bfloat16)
        send_all(
            lambda peer: out_send.at[c, peer_rows(peer), :],
            out_recv.at[c, own, :],
            out_send_sem.at[c],
            out_recv_sem.at[c],
        )
        out_recv[c, own, :] = out_send[c, own, :]
        return carry

    lax.fori_loop(0, chunks, expand, 0)

    small[1].wait()
    small[2].wait()
    wait_all(page_recv.at[others, :], page_sems.at[1])
    pages = page_recv[...]
    latent = pages.shape[1] - ROPE
    transposed = (((1,), (1,)), ((), ()))
    holder = div(iota((1, n * TILE), 1), TILE)
    owner = jnp.zeros((1, n * TILE), jnp.int32)
    for p in range(n):
        owner = jnp.where(holder == p, owner_ref[0, p], owner)
    for r in range(rows):
        query = queries_buf[r]
        cache = cache_buf[r]
        page_scores = (
            lax.dot_general(query, pages, transposed, preferred_element_type=jnp.float32)
            * score_scale
        )
        page_scores = jnp.where(owner == r, page_scores, -jnp.inf)
        local_scores = (
            lax.dot_general(query, cache, transposed, preferred_element_type=jnp.float32)
            * score_scale
        )
        position = iota((1, cache.shape[0]), 1)
        local_scores = jnp.where(position < lengths_ref[r], local_scores, -jnp.inf)
        peak = jnp.maximum(
            jnp.max(page_scores, axis=1, keepdims=True), jnp.max(local_scores, axis=1, keepdims=True)
        )
        page_exp = jnp.exp(page_scores - peak)
        local_exp = jnp.exp(local_scores - peak)
        total = jnp.sum(page_exp, axis=1, keepdims=True) + jnp.sum(local_exp, axis=1, keepdims=True)
        attn_ref[r] = (
            jnp.dot(
                (page_exp / total).astype(jnp.bfloat16),
                pages[:, :latent],
                preferred_element_type=jnp.float32,
            )
            + jnp.dot(
                (local_exp / total).astype(jnp.bfloat16),
                cache[:, :latent],
                preferred_element_type=jnp.float32,
            )
        ).astype(jnp.bfloat16)

    table = (TILE, n * TILE)
    row_of = div(iota(table, 0), subs)
    expert_of = div(div(iota(table, 1), TILE), n // EXPERTS)
    weight = jnp.zeros(table, jnp.float32)
    for k in range(routes_ref.shape[1]):
        route = jnp.zeros(table, jnp.int32)
        mix = jnp.zeros(table, jnp.float32)
        for r in range(rows):
            route = jnp.where(row_of == r, routes_ref[r, k], route)
            mix = jnp.where(row_of == r, mix_ref[r, k], mix)
        weight += jnp.where(route == expert_of, mix, 0.0)
    weight = jnp.where(iota(table, 0) == mod(iota(table, 1), TILE), weight, 0.0)
    high = weight.astype(jnp.bfloat16)
    low = (weight - high.astype(jnp.float32)).astype(jnp.bfloat16)
    for c in range(chunks):
        wait_all(out_recv.at[c, others, :], out_recv_sem.at[c])
        got = out_recv[c]
        mixed = jnp.dot(high, got, preferred_element_type=jnp.float32) + jnp.dot(
            low, got, preferred_element_type=jnp.float32
        )
        for r in range(rows):
            for q in range(subs):
                out_wide[r : r + 1, c * chunk + q * LANES : c * chunk + (q + 1) * LANES] = mixed[
                    r * subs + q : r * subs + q + 1, :
                ]
    moe_ref[...] = (hidden_ref[...].astype(jnp.float32) + out_wide[...]).astype(jnp.bfloat16)

    wait_all(ids_recv.at[pl.ds(0, n - 1)], ids_sems.at[0])
    wait_all(row_recv.at[others, :], row_sems.at[0])
    wait_all(page_send.at[others, :], page_sems.at[0])
    for c in range(chunks):
        wait_all(out_send.at[c, others, :], out_send_sem.at[c])


def per_device(
    sizes,
    hidden,
    norm_gain,
    routes,
    gate_weights,
    w_gate,
    w_up,
    w_down,
    queries,
    local_cache,
    cache_lengths,
    swap_pool,
    page_ids,
    page_owner,
):
    n = sizes[0] * sizes[1]
    rows, width = hidden.shape
    total = rows * n
    hidden_units = w_gate.shape[1]
    channels = queries.shape[2]
    subs = TILE // rows
    part = width // subs
    chunk = subs * LANES
    chunks = width // chunk
    id_lanes = -(-n // LANES) * LANES
    vmem = pl.BlockSpec(memory_space=pltpu.VMEM)
    smem = pl.BlockSpec(memory_space=pltpu.SMEM)
    hbm = pl.BlockSpec(memory_space=pl.ANY)
    bf16, f32 = jnp.bfloat16, jnp.float32
    dma = pltpu.SemaphoreType.DMA
    return pl.pallas_call(
        functools.partial(layer_kernel, sizes),
        out_shape=(
            jax.ShapeDtypeStruct(queries.shape[:2] + (channels - ROPE,), bf16),
            jax.ShapeDtypeStruct(hidden.shape, bf16),
        ),
        in_specs=[vmem] * 3 + [smem] * 4 + [hbm] * 6,
        out_specs=(vmem, vmem),
        scratch_shapes=[
            pltpu.VMEM((AHEAD, part, hidden_units), bf16),
            pltpu.VMEM((AHEAD, part, hidden_units), bf16),
            pltpu.VMEM((chunks, hidden_units, chunk), bf16),
            pltpu.VMEM(queries.shape, bf16),
            pltpu.VMEM(local_cache.shape, bf16),
            pltpu.VMEM(swap_pool.shape, bf16),
            pltpu.VMEM((TILE, part), f32),
            pltpu.VMEM((TILE, part), bf16),
            pltpu.VMEM((n * TILE, part), bf16),
            pltpu.VMEM((subs, total, part), bf16),
            pltpu.VMEM((total, hidden_units), f32),
            pltpu.VMEM((total, hidden_units), f32),
            pltpu.VMEM((total, hidden_units), bf16),
            pltpu.VMEM((8, id_lanes), jnp.int32),
            pltpu.VMEM((n, 8, id_lanes), jnp.int32),
            pltpu.VMEM((n * TILE, channels), bf16),
            pltpu.VMEM((n * TILE, channels), bf16),
            pltpu.VMEM((chunks, n * TILE, LANES), bf16),
            pltpu.VMEM((chunks, n * TILE, LANES), bf16),
            pltpu.VMEM((rows, width), f32),
            dma((AHEAD,)),
            dma((AHEAD,)),
            dma((chunks,)),
            dma((3,)),
            dma((2,)),
            dma((2,)),
            dma((2,)),
            dma((chunks,)),
            dma((chunks,)),
        ],
        compiler_params=pltpu.CompilerParams(
            collective_id=0, has_side_effects=True, vmem_limit_bytes=63 * 1024 * 1024
        ),
    )(
        hidden,
        norm_gain.reshape(1, -1),
        page_ids,
        routes,
        gate_weights,
        cache_lengths,
        page_owner,
        queries,
        local_cache,
        swap_pool,
        w_gate,
        w_up,
        w_down,
    )


def solution(mesh):
    in_specs = (
        P(("group", "role", "dev"), None),
        P(),
        P(("group", "role", "dev"), None),
        P(("group", "role", "dev"), None),
        P(None, ("role", "dev")),
        P(None, ("role", "dev")),
        P(("role", "dev"), None),
        P(("group", "role", "dev"), None, None),
        P(("group", "role", "dev"), None, None),
        P(("group", "role", "dev")),
        P(("group", "role", "dev"), None, None),
        P(("group", "role", "dev"), None),
        P(("group", "role", "dev"), None),
    )
    out_specs = (P(("group", "role", "dev"), None, None), P(("group", "role", "dev"), None))
    sizes = (mesh.shape["role"], mesh.shape["dev"])
    return jax.shard_map(
        functools.partial(per_device, sizes),
        mesh=mesh,
        in_specs=in_specs,
        out_specs=out_specs,
        check_vma=False,
    )
```

time: 108 us -> 60.4 us (0.56)
  Pallas kernels: 0 us -> 55.2 us
  matrix products: 42.1 us -> 0 us
  waiting for transfers between devices: 27.6 us -> 0 us
  starting transfers between devices: 22.8 us -> 0 us
  other arithmetic: 5.31 us -> 0 us
  local copies, waits for them, and re-layouts: 8.41 us -> 4.28 us
    pallas_call x0 -> x1, Pallas kernels: none -> 55.2 us  [per_device(): pl.pallas_call(functools.partial(layer_kernel, sizes), out_shape=(jax.Sha...]
    dot_general x9 -> x0, matrix products: 42.1 us -> none  [the longest x1 20.8 us: expert_block(): output = jnp.dot(act_units, w_down, preferred_element_type=jnp.float32)]
    all_to_all x4 -> x0, waiting for transfers between devices: 27.6 us -> none  [the longest x1 17.6 us: per_device(): lax.all_to_all(partial_out, ('role', 'dev'), split_axis=0, concat_axis=0,...]
    all_to_all x4 -> x0, starting transfers between devices: 22.8 us -> none  [the longest x1 7.36 us: per_device(): lax.all_to_all(page_ids.reshape(-1), ('role', 'dev'), split_axis=0, conca...]
    gather x4 -> x0, local copies, waits for them, and re-layouts: 4.13 us -> none  [the longest x1 1.7 us: device_attention(): page_query = queries[owners]]
    unnamed x6 -> x2, local copies, waits for them, and re-layouts: 0.02 us -> 2.94 us
    reduce_sum x5 -> x0, other arithmetic: 1.87 us -> none  [the longest x1 0.92 us: per_device(): jnp.mean(hidden_wide * hidden_wide, axis=1, keepdims=True) + norm_eps]
    all_to_all x1 -> x0, local copies, waits for them, and re-layouts: 1.38 us -> none  [per_device(): lax.all_to_all(page_ids.reshape(-1), ('role', 'dev'), split_axis=0, conca...]
  transfers between devices with their start and end apart: 4 -> 0, of which waited for: 2 -> 0; matrix products, arithmetic and copies ran while one was open for 49% -> 0% of each run, Pallas kernels for 0% -> 0%
where the time goes in v1:
time: 60.4 us; the launch traced here: 60.1 us
  Pallas kernels  55.2 us (91%)
  local copies, waits for them, and re-layouts  4.28 us (7%)
  between operations  0.64 us (1%)
    pallas_call x1, Pallas kernels, per_device(): pl.pallas_call(functools.partial(layer_kernel, sizes), out_shape=(jax.Sha...  55.2 us
    unnamed x2, local copies, waits for them, and re-layouts  2.94 us
    reshape x1, local copies, waits for them, and re-layouts, per_device(): norm_gain.reshape(1, -1)  1.34 us

profile of v1, /device:TPU:0, one launch (start us, length us, event | category | flops | bytes accessed | tf_op | source)
XLA Modules:
  0.0 60.1 jit_solution(15744421992427948054)
XLA Ops:
  0.6 1.3 %reshape.7.gain_ref = bf16[1,7168]{1,0:T(2,128)(2,1)} reshape(bf16[7168]{0:T(1024)(128)(2,1)} %param.14) | data formatting | bytes 28672 | tf_op jit(solution)/shard_map/reshape | solution.py:431
  2.0 55.2 %shard_map.140 = (bf16[2,64,512]{2,1,0:T(8,128)(2,1)}, bf16[2,7168]{1,0:T(2,128)(2,1)}) custom-call(bf16[2,7168]{1,0:T(2,128)(2,1)} %hidden_ref.1, bf16[1,7168]{1,0:T(2,128)(2,1)} %reshape.7.gain_ref, s32[1,16]{1,0:T(1,128)} %ids_ref.1, s32[2,8]{1,0:T(2,128)} %routes_ref.1, f32[2,8]{1,0:T(2,128)} %mix_ref.1, s32[2]{0:T(128)} %lengths_ref.1, ...), custom_call_target="tpu_custom_call" | custom-call | tf_op jit(solution)/shard_map/pallas_call | solution.py:387
  57.1 1.6 %copy.17 = bf16[2,64,512]{2,1,0:T(8,128)(2,1)} copy(bf16[2,64,512]{2,1,0:T(8,128)(2,1)} %get-tuple-element.4) | data formatting | bytes 262144
  58.7 1.4 %copy.18 = bf16[2,7168]{1,0:T(2,128)(2,1)} copy(bf16[2,7168]{1,0:T(2,128)(2,1)} %get-tuple-element.5) | data formatting | bytes 57344

commit v2 on v1

--- a/solution.py
+++ b/solution.py
@@ -86,7 +86,8 @@
     chunks = width // chunk
     block = min(n, 16)
     block_rows = block * rows
-    me = lax.axis_index("role") * devs + lax.axis_index("dev")
+    my_role, my_dev = lax.axis_index("role"), lax.axis_index("dev")
+    me = my_role * devs + my_dev
 
     def target(step):
         peer = lax.rem(me + step, n)
@@ -141,10 +142,10 @@
         down_copy(c).start()
 
     ids_send[...] = jnp.zeros_like(ids_send)
-    ids_send[:, 0:n] = jnp.broadcast_to(ids_ref[...], (8, n))
+    ids_send[:, 0:n] = ids_ref[...]
     hidden_wide = hidden_ref[...].astype(jnp.float32)
     inv_rms = lax.rsqrt(jnp.mean(hidden_wide * hidden_wide, axis=1, keepdims=True) + norm_eps)
-    normed = hidden_wide * inv_rms * gain_ref[...].astype(jnp.float32)
+    normed = hidden_wide * inv_rms * gain_ref[...].astype(jnp.float32).reshape(1, width)
     for r in range(rows):
         for s in range(subs):
             packed[r * subs + s : r * subs + s + 1, :] = normed[r : r + 1, s * part : (s + 1) * part]
@@ -174,7 +175,21 @@
 
     others = pl.ds(0, (n - 1) * TILE)
     send_all(lambda peer: ids_send, ids_recv.at[me], ids_sems.at[0], ids_sems.at[1])
-    send_all(lambda peer: row_send, row_recv.at[own, :], row_sems.at[0], row_sems.at[1])
+
+    def send_rows(step, carry):
+        pltpu.make_async_remote_copy(
+            src_ref=row_send,
+            dst_ref=row_recv.at[own, :],
+            send_sem=row_sems.at[0],
+            recv_sem=row_sems.at[1],
+            device_id={"dev": lax.rem(my_dev + step, devs)},
+            device_id_type=pl.DeviceIdType.MESH,
+        ).start()
+        return carry
+
+    lax.fori_loop(1, devs, send_rows, 0)
+    crossed = row_recv.at[pl.ds(0, (devs - 1) * TILE), :]
+    shared = row_recv.at[pl.ds(0, (roles - 1) * devs * TILE), :]
 
     def peer_rows(peer):
         return pl.ds(pl.multiple_of(peer * TILE, TILE), TILE)
@@ -183,7 +198,7 @@
     wait_all(ids_recv.at[pl.ds(0, n - 1)], ids_sems.at[1])
     ids_all = ids_recv[...]
     wanted = jnp.sum(jnp.where(iota(ids_all.shape, 2) == me, ids_all, 0), axis=2, keepdims=True)
-    wanted = jnp.concatenate([wanted, wanted], axis=1).reshape(n * TILE, 1)
+    wanted = jnp.broadcast_to(wanted, (n, TILE, 1)).reshape(n * TILE, 1)
     pool_rows = pool_buf[...].reshape(-1, pool_buf.shape[2])
     pick = (n * TILE, pool_rows.shape[0])
     chosen = (wanted == div(iota(pick, 1), TILE)) & (
@@ -194,6 +209,25 @@
         pool_rows,
         preferred_element_type=jnp.float32,
     ).astype(jnp.bfloat16)
+    square = (block * TILE, block * TILE)
+
+    def place(index):
+        return mod(index, block_rows) * subs + div(index, block_rows)
+
+    to_parts = jnp.where(place(iota(square, 0)) == iota(square, 1), 1.0, 0.0).astype(jnp.bfloat16)
+    to_packed = jnp.where(iota(square, 0) == place(iota(square, 1)), 1.0, 0.0).astype(jnp.bfloat16)
+
+    wait_all(crossed, row_sems.at[1])
+    mine = pl.ds(pl.multiple_of(my_role * devs * TILE, TILE), devs * TILE)
+    for step in range(1, roles):
+        pltpu.make_async_remote_copy(
+            src_ref=row_recv.at[mine, :],
+            dst_ref=row_recv.at[mine, :],
+            send_sem=row_sems.at[2],
+            recv_sem=row_sems.at[3],
+            device_id={"role": lax.rem(my_role + step, roles)},
+            device_id_type=pl.DeviceIdType.MESH,
+        ).start()
     send_all(
         lambda peer: page_send.at[peer_rows(peer), :],
         page_recv.at[own, :],
@@ -201,16 +235,7 @@
         page_sems.at[1],
     )
     page_recv[own, :] = page_send[own, :]
-
-    square = (block * TILE, block * TILE)
-
-    def place(index):
-        return mod(index, block_rows) * subs + div(index, block_rows)
-
-    to_parts = jnp.where(place(iota(square, 0)) == iota(square, 1), 1.0, 0.0).astype(jnp.bfloat16)
-    to_packed = jnp.where(iota(square, 0) == place(iota(square, 1)), 1.0, 0.0).astype(jnp.bfloat16)
-
-    wait_all(row_recv.at[others, :], row_sems.at[1])
+    wait_all(shared, row_sems.at[3])
     for b in range(n // block):
         moved = jnp.dot(
             to_parts,
@@ -347,10 +372,16 @@
     moe_ref[...] = (hidden_ref[...].astype(jnp.float32) + out_wide[...]).astype(jnp.bfloat16)
 
     wait_all(ids_recv.at[pl.ds(0, n - 1)], ids_sems.at[0])
-    wait_all(row_recv.at[others, :], row_sems.at[0])
+    wait_all(crossed, row_sems.at[0])
+    wait_all(shared, row_sems.at[2])
     wait_all(page_send.at[others, :], page_sems.at[0])
     for c in range(chunks):
         wait_all(out_send.at[c, others, :], out_send_sem.at[c])
+
+
+def hand_on(attn_ref, moe_ref, attn_out, moe_out):
+    attn_out[...] = attn_ref[...]
+    moe_out[...] = moe_ref[...]
 
 
 def per_device(
@@ -384,7 +415,7 @@
     hbm = pl.BlockSpec(memory_space=pl.ANY)
     bf16, f32 = jnp.bfloat16, jnp.float32
     dma = pltpu.SemaphoreType.DMA
-    return pl.pallas_call(
+    attn_out, moe_out = pl.pallas_call(
         functools.partial(layer_kernel, sizes),
         out_shape=(
             jax.ShapeDtypeStruct(queries.shape[:2] + (channels - ROPE,), bf16),
@@ -406,8 +437,8 @@
             pltpu.VMEM((total, hidden_units), f32),
             pltpu.VMEM((total, hidden_units), f32),
             pltpu.VMEM((total, hidden_units), bf16),
-            pltpu.VMEM((8, id_lanes), jnp.int32),
-            pltpu.VMEM((n, 8, id_lanes), jnp.int32),
+            pltpu.VMEM((1, id_lanes), jnp.int32),
+            pltpu.VMEM((n, 1, id_lanes), jnp.int32),
             pltpu.VMEM((n * TILE, channels), bf16),
             pltpu.VMEM((n * TILE, channels), bf16),
             pltpu.VMEM((chunks, n * TILE, LANES), bf16),
@@ -418,7 +449,7 @@
             dma((chunks,)),
             dma((3,)),
             dma((2,)),
-            dma((2,)),
+            dma((4,)),
             dma((2,)),
             dma((chunks,)),
             dma((chunks,)),
@@ -428,7 +459,7 @@
         ),
     )(
         hidden,
-        norm_gain.reshape(1, -1),
+        norm_gain,
         page_ids,
         routes,
         gate_weights,
@@ -441,6 +472,15 @@
         w_up,
         w_down,
     )
+    return pl.pallas_call(
+        hand_on,
+        out_shape=(
+            jax.ShapeDtypeStruct(attn_out.shape, bf16),
+            jax.ShapeDtypeStruct(moe_out.shape, bf16),
+        ),
+        in_specs=[vmem, vmem],
+        out_specs=(vmem, vmem),
+    )(attn_out, moe_out)
 
 
 def solution(mesh):

time: 60.4 us -> 49.1 us (0.81)
  Pallas kernels: 55.2 us -> 48.2 us
  local copies, waits for them, and re-layouts: 4.28 us -> 0 us
    pallas_call x1, Pallas kernels: 55.2 us -> 46.7 us  [per_device(): pl.pallas_call(functools.partial(layer_kernel, sizes), out_shape=(jax.Sha...]
    unnamed x2 -> x0, local copies, waits for them, and re-layouts: 2.94 us -> none
    pallas_call x0 -> x1, Pallas kernels: none -> 1.57 us  [per_device(): pl.pallas_call(hand_on, out_shape=(jax.ShapeDtypeStruct(attn_out.shape, b...]
    reshape x1 -> x0, local copies, waits for them, and re-layouts: 1.34 us -> none  [per_device(): norm_gain.reshape(1, -1)]
where the time goes in v2:
time: 49.1 us; the launch traced here: 48.9 us
  Pallas kernels  48.2 us (98%)
  between operations  0.64 us (1%)
    pallas_call x1, Pallas kernels, per_device(): pl.pallas_call(functools.partial(layer_kernel, sizes), out_shape=(jax.Sha...  46.7 us
    pallas_call x1, Pallas kernels, per_device(): pl.pallas_call(hand_on, out_shape=(jax.ShapeDtypeStruct(attn_out.shape, b...  1.57 us

profile of v2, /device:TPU:0, one launch (start us, length us, event | category | flops | bytes accessed | tf_op | source)
XLA Modules:
  0.0 48.9 jit_solution(4608909941480097595)
XLA Ops:
  0.6 46.7 %shard_map.140 = (bf16[2,64,512]{2,1,0:T(8,128)(2,1)}, bf16[2,7168]{1,0:T(2,128)(2,1)}) custom-call(bf16[2,7168]{1,0:T(2,128)(2,1)} %hidden_ref.1, bf16[7168]{0:T(1024)(128)(2,1)} %gain_ref.1, s32[1,16]{1,0:T(1,128)} %ids_ref.1, s32[2,8]{1,0:T(2,128)} %routes_ref.1, f32[2,8]{1,0:T(2,128)} %mix_ref.1, s32[2]{0:T(128)} %lengths_ref.1, s32[1,16]{1,0:T(1,128)} %owner_ref.1, ...), custom_call_target="tpu_custom_call" | custom-call | tf_op jit(solution)/shard_map/pallas_call | solution.py:418
  47.3 1.6 %shard_map.141 = (bf16[2,64,512]{2,1,0:T(8,128)(2,1)}, bf16[2,7168]{1,0:T(2,128)(2,1)}) custom-call(bf16[2,64,512]{2,1,0:T(8,128)(2,1)} %get-tuple-element.4.attn_ref, bf16[2,7168]{1,0:T(2,128)(2,1)} %get-tuple-element.5.moe_ref), custom_call_target="tpu_custom_call" | custom-call | tf_op jit(solution)/shard_map/pallas_call | solution.py:475
